TPU v7x, 32 devices: a whole 2x2x4 slice. The times are simulated.
32 devices in a mesh: grp: 2 (over y), seq: 8 (over z, x), fsdp: 2 (over core).
Axes of the slice: x: 2, y: 2, z: 4, core: 2. Of those that a mesh axis runs over, the one named last changes fastest.
Arguments:
- base_codes: int32 [4, 4096], P(('grp', 'fsdp'), 'seq'), parts along dimension 0, may hold values from 0 to 3
- stem_weight: bfloat16 [15, 4, 1536], replicated, may hold values from -1.5 to 1.5
- norm_gains: float32 [2, 1536], replicated, may hold values from 0.1 to 1.9
- conv_weight: bfloat16 [2, 1536, 3, 384], P(None, 'fsdp'), may hold values from -0.09375 to 0.09375
- point_weight: bfloat16 [2, 1536, 384], P(None, 'fsdp'), may hold values from -0.3125 to 0.3125
- cotangent: bfloat16 [4, 1536, 2048], P(('grp', 'fsdp'), 'seq'), parts along dimension 0, may hold values from -0.29882812 to 0.29882812
Outputs:
- pooled: bfloat16 [4, 1536, 2048], P(('grp', 'fsdp'), 'seq'), parts along dimension 0
- saliency: float32 [4, 4, 4096], P(('grp', 'fsdp'), None, 'seq'), parts along dimension 0
There are 2 independent parts, one for each index of `grp`. A program takes and returns all parts, laid end to end along the dimension named above; an argument that names none is the same for every part. Nothing has to cross between parts.
All inputs are finite; a program needn't handle non-finite values.
Results may differ from a plain program's by a relative error of at most 0.0055.
Values may be sent and summed in bfloat16 or wider, within the bound.
A program may use at most 128 MiB of HBM per device.

v0:
```python
import jax
import jax.numpy as jnp
from jax import lax
from jax.sharding import PartitionSpec as P

FIRST_DILATION = 32
POOL = 2


def with_halo(block, sides, width):
    for axis, dim in sides:
        count = lax.axis_size(axis)
        forward = [(i, i + 1) for i in range(count - 1)]
        backward = [(target, source) for source, target in forward]
        low = lax.ppermute(
            lax.slice_in_dim(block, block.shape[dim] - width, None, axis=dim), axis, forward
        )
        high = lax.ppermute(lax.slice_in_dim(block, 0, width, axis=dim), axis, backward)
        block = jnp.concatenate([low, block, high], axis=dim)
    return block


def rms_gain(hidden, gain_row):
    inv_rms = lax.rsqrt(jnp.mean(hidden * hidden, axis=-1, keepdims=True) + 1e-06)
    return hidden * inv_rms * gain_row


def activate(hidden, gain_row):
    return jax.nn.gelu(rms_gain(hidden, gain_row))


def through_norm(hidden, gain_row, gradient):
    _, pullback = jax.vjp(lambda inputs: activate(inputs, gain_row), hidden)
    return pullback(gradient)[0]


def through_gelu(conv_out, gradient):
    _, pullback = jax.vjp(jax.nn.gelu, conv_out)
    return pullback(gradient)[0]


def stem_rows(wide_codes, code_inside, stem_weight):
    stem_taps = stem_weight.shape[0]
    base_count = stem_weight.shape[1]
    out_rows = wide_codes.shape[0] - (stem_taps - 1)
    onehot = (
        (wide_codes[:, None] == lax.iota(jnp.int32, base_count)[None, :]).astype(jnp.float32)
        * code_inside
    ).astype(jnp.bfloat16)
    stacked = jnp.concatenate(
        [
            lax.slice_in_dim(onehot, tap_index, tap_index + out_rows, axis=0)
            for tap_index in range(stem_taps)
        ],
        axis=1,
    )
    stem_flat = stem_weight.reshape(stem_taps * base_count, stem_weight.shape[2])
    return jnp.dot(stacked, stem_flat, preferred_element_type=jnp.float32)


def taps_forward(padded, convolution_result, dilation_rate):
    tap_count = convolution_result.shape[1]
    out_rows = padded.shape[0] - 2 * (tap_count // 2) * dilation_rate
    summed = jnp.zeros((out_rows, convolution_result.shape[2]), jnp.float32)
    for tap_index in range(tap_count):
        window = lax.slice_in_dim(
            padded, tap_index * dilation_rate, tap_index * dilation_rate + out_rows, axis=0
        )
        summed = summed + jnp.dot(
            window, convolution_result[:, tap_index, :], preferred_element_type=jnp.float32
        )
    return summed


def taps_backward(padded, convolution_result, dilation_rate):
    tap_count = convolution_result.shape[1]
    out_rows = padded.shape[0] - 2 * (tap_count // 2) * dilation_rate
    summed = jnp.zeros((out_rows, convolution_result.shape[0]), jnp.float32)
    for tap_index in range(tap_count):
        first_row = (tap_count - 1 - tap_index) * dilation_rate
        window = lax.slice_in_dim(padded, first_row, first_row + out_rows, axis=0)
        summed = summed + lax.dot_general(
            window,
            convolution_result[:, tap_index, :],
            (((1,), (1,)), ((), ())),
            preferred_element_type=jnp.float32,
        )
    return summed


def fetch_panels(conv_weight, point_weight, layer_number_index):
    return (
        lax.all_gather(conv_weight[layer_number_index], "fsdp", axis=0, tiled=True),
        lax.all_gather(point_weight[layer_number_index], "fsdp", axis=0, tiled=True),
    )


def body(base_codes, stem_weight, norm_gains, conv_weight, point_weight, cotangent):
    sequence_codes = base_codes[0]
    shard_local_rows = sequence_codes.shape[0]
    layer_count = norm_gains.shape[0]
    stem_taps = stem_weight.shape[0]
    base_count = stem_weight.shape[1]
    stem_half = stem_taps // 2
    wide_codes = with_halo(sequence_codes, (("seq", 0),), stem_half)
    position = (
        lax.axis_index("seq") * shard_local_rows
        - stem_half
        + lax.iota(jnp.int32, shard_local_rows + 2 * stem_half)
    )
    code_inside = ((position >= 0) & (position < shard_local_rows * lax.axis_size("seq"))).astype(
        jnp.float32
    )[:, None]
    hidden = stem_rows(wide_codes, code_inside, stem_weight)
    kept_panels = []
    stored = []
    for layer_number_index in range(layer_count):
        dilation_rate = FIRST_DILATION * 2**layer_number_index
        weights_now = fetch_panels(conv_weight, point_weight, layer_number_index)
        kept_panels.append(weights_now)
        convolution_result, point_full = weights_now
        activation = activate(hidden, norm_gains[layer_number_index])
        padded = with_halo(activation.astype(jnp.bfloat16), (("seq", 0),), dilation_rate)
        conv_out = taps_forward(padded, convolution_result, dilation_rate)
        bottleneck = jax.nn.gelu(conv_out).astype(jnp.bfloat16)
        branch = lax.dot_general(
            bottleneck, point_full, (((1,), (1,)), ((), ())), preferred_element_type=jnp.float32
        )
        stored.append((hidden, conv_out))
        hidden = hidden + branch
    pooled = jnp.mean(hidden.reshape(shard_local_rows // POOL, POOL, hidden.shape[1]), axis=1)
    flipped = pooled.T.astype(jnp.bfloat16)
    out_pooled = lax.all_to_all(flipped, "seq", split_axis=0, concat_axis=1, tiled=True)[None]
    arrived = lax.all_to_all(cotangent[0], "seq", split_axis=1, concat_axis=0, tiled=True)
    spread = arrived.T.astype(jnp.float32) / POOL
    gradient = jnp.broadcast_to(
        spread[:, None, :], (shard_local_rows // POOL, POOL, spread.shape[1])
    ).reshape(shard_local_rows, spread.shape[1])
    for layer_number_index in reversed(range(layer_count)):
        dilation_rate = FIRST_DILATION * 2**layer_number_index
        convolution_result, point_full = kept_panels[layer_number_index]
        start_hidden, conv_out = stored[layer_number_index]
        bottleneck_gradient = jnp.dot(
            gradient.astype(jnp.bfloat16), point_full, preferred_element_type=jnp.float32
        )
        convolution_gradient = through_gelu(conv_out, bottleneck_gradient).astype(jnp.bfloat16)
        padded = with_halo(convolution_gradient, (("seq", 0),), dilation_rate)
        grad_activation = taps_backward(padded, convolution_result, dilation_rate)
        gradient = gradient + through_norm(
            start_hidden, norm_gains[layer_number_index], grad_activation
        )
    stem_flat = stem_weight.reshape(stem_taps * base_count, stem_weight.shape[2]).astype(
        jnp.float32
    )
    output_projection = lax.dot_general(
        stem_flat, gradient, (((1,), (1,)), ((), ())), precision=lax.Precision.HIGHEST
    )
    widened = with_halo(output_projection.astype(jnp.bfloat16), (("seq", 1),), stem_half).astype(
        output_projection.dtype
    )
    folded = widened.reshape(stem_taps, base_count, shard_local_rows + 2 * stem_half)
    saliency = jnp.zeros((base_count, shard_local_rows), jnp.float32)
    for tap_index in range(stem_taps):
        first_col = stem_taps - 1 - tap_index
        saliency = saliency + lax.slice_in_dim(
            folded[tap_index], first_col, first_col + shard_local_rows, axis=1
        )
    return (out_pooled, saliency[None])


def solution(mesh):
    in_specs = (
        P(("grp", "fsdp"), "seq"),
        P(),
        P(),
        P(None, "fsdp", None, None),
        P(None, "fsdp", None),
        P(("grp", "fsdp"), "seq", None),
    )
    out_specs = (P(("grp", "fsdp"), "seq", None), P(("grp", "fsdp"), None, "seq"))
    return jax.shard_map(body, mesh=mesh, in_specs=in_specs, out_specs=out_specs, check_vma=False)
```

profile of v0, /device:TPU:10, one launch (start us, length us, event | category | flops | bytes accessed | tf_op | source)
XLA Modules:
  0.0 178.3 jit_solution(6379252027287366788)
XLA Ops:
  7.2 4.2 %fusion.115 = (bf16[1,768,3,384]{3,1,2,0:T(8,128)(2,1)}, bf16[1,768,3,384]{3,1,2,0:T(8,128)(2,1)}) fusion(bf16[2,768,3,384]{3,1,2,0:T(8,128)(2,1)} %param.9), kind=kLoop, calls=%fused_computation.169 | loop fusion | bytes 7077888 | tf_op jit(solution)/shard_map/slice | solution.py:93
  13.5 3.4 %collective-permute-start = (s32[7]{0:T(128)S(1)}, s32[7]{0:T(128)S(1)}, u32[]{:S(2)}, u32[]{:S(2)}) collective-permute-start(s32[7]{0:T(128)S(1)} %get-tuple-element.33), channel_id=1, source_target_pairs={{0,2},{2,4},{4,6},{6,8},{8,10},{10,12},{12,14},{1,3},{3,5},{5,7},{... | collective-permute-start | bytes 92 | tf_op jit(solution)/shard_map/ppermute | solution.py:15
  20.6 6.2 %all-to-all-start.1 = ((bf16[192,8,256]{2,0,1:T(8,128)(2,1)}), bf16[192,8,256]{2,0,1:T(8,128)(2,1)}, u32[]{:S(2)}, u32[]{:S(2)}) async-start(bf16[192,8,256]{2,0,1:T(8,128)(2,1)} %copy.14), calls=%async_computation.1 | async-start | bytes 1572864 | tf_op jit(solution)/shard_map/all_to_all | solution.py:134
  32.7 3.4 %collective-permute-start.2 = (bf16[32,1536]{1,0:T(8,128)(2,1)S(1)}, bf16[32,1536]{1,0:T(8,128)(2,1)S(1)}, u32[]{:S(2)}, u32[]{:S(2)}) collective-permute-start(bf16[32,1536]{1,0:T(8,128)(2,1)S(1)} %get-tuple-element.8), channel_id=1, source_target_pairs={{0,2},{2,4},{4,6},{6,8},{8,10},{10,12},{12,14},{1,3},{3,5},{5,7},{... | collective-permute-start | bytes 294920 | tf_op jit(solution)/shard_map/ppermute | solution.py:15
  38.8 4.5 %all-to-all-done.1 = bf16[192,8,256]{2,0,1:T(8,128)(2,1)} async-done(((bf16[192,8,256]{2,0,1:T(8,128)(2,1)}), bf16[192,8,256]{2,0,1:T(8,128)(2,1)}, u32[]{:S(2)}, u32[]{:S(2)}) %all-to-all-start.1) | async-done | bytes 786464 | tf_op jit(solution)/shard_map/all_to_all | solution.py:134
  45.8 3.2 %copy.15 = f32[256,1536]{1,0:T(8,128)} copy(f32[256,1536]{0,1:T(8,128)} %bitcast.74) | data formatting | bytes 3145728 | tf_op jit(solution)/shard_map/div | solution.py:135
  49.0 4.5 %broadcast_in_dim.11 = f32[256,2,1536]{2,1,0:T(2,128)} broadcast(f32[256,1536]{1,0:T(8,128)} %copy.15), dimensions={0,2} | broadcast | bytes 4718592 | tf_op jit(solution)/shard_map/broadcast_in_dim | solution.py:136
  53.4 5.2 %reshape.102 = f32[512,1536]{1,0:T(8,128)} reshape(f32[256,2,1536]{2,1,0:T(2,128)} %broadcast_in_dim.11) | data formatting | bytes 6291456 | tf_op jit(solution)/shard_map/reshape | solution.py:138
  58.7 2.9 %fusion.51 = f32[512,384]{1,0:T(8,128)S(1)} fusion(bf16[512,1536]{1,0:T(8,128)(2,1)} %copy-done.6, bf16[1536,3,384]{2,0,1:T(8,128)(2,1)} %bitcast.77), kind=kOutput, calls=%fused_computation.80 | convolution fusion | flops 603979776 | bytes 3538944 | tf_op jit(solution)/shard_map/dot_general | solution.py:69
  72.8 4.9 %collective-permute-start.4 = (bf16[64,1536]{1,0:T(8,128)(2,1)S(1)}, bf16[64,1536]{1,0:T(8,128)(2,1)}, u32[]{:S(2)}, u32[]{:S(2)}) collective-permute-start(bf16[64,1536]{1,0:T(8,128)(2,1)S(1)} %get-tuple-element.6), channel_id=1, source_target_pairs={{0,2},{2,4},{4,6},{6,8},{8,10},{10,12},{12,14},{1,3},{3,5},{5,7},{... | collective-permute-start | bytes 589832 | tf_op jit(solution)/shard_map/ppermute | solution.py:15
  79.7 2.9 %fusion.54 = f32[512,384]{1,0:T(8,128)S(1)} fusion(bf16[512,1536]{1,0:T(8,128)(2,1)} %copy-done.4, bf16[1536,3,384]{2,0,1:T(8,128)(2,1)} %bitcast.83), kind=kOutput, calls=%fused_computation.83 | convolution fusion | flops 603979776 | bytes 3538944 | tf_op jit(solution)/shard_map/dot_general | solution.py:69
  82.5 3.7 %collective-permute-done.5 = bf16[64,1536]{1,0:T(8,128)(2,1)} collective-permute-done((bf16[64,1536]{1,0:T(8,128)(2,1)S(1)}, bf16[64,1536]{1,0:T(8,128)(2,1)}, u32[]{:S(2)}, u32[]{:S(2)}) %collective-permute-start.5) | collective-permute-done | bytes 196640 | tf_op jit(solution)/shard_map/ppermute | solution.py:18
  91.0 3.8 %fusion.69 = bf16[512,384]{1,0:T(8,128)(2,1)S(1)} fusion(f32[512,384]{1,0:T(8,128)} %fusion.39, bf16[1,1536,384]{2,1,0:T(8,128)(2,1)} %all-gather.15.cloned.1.call-done, f32[512,1536]{1,0:T(8,128)} %reshape.102), kind=kOutput, calls=%fused_computation.98 | convolution fusion | flops 608698368 | bytes 5505024 | tf_op jit(solution)/shard_map/dot_general | solution.py:143
  95.5 4.3 %fusion.53 = f32[512,1536]{1,0:T(8,128)} fusion(bf16[512,384]{1,0:T(8,128)(2,1)S(1)} %fusion.69, bf16[1536,3,384]{2,0,1:T(8,128)(2,1)} %bitcast.84), kind=kOutput, calls=%fused_computation.82 | convolution fusion | flops 603979776 | bytes 4718592 | tf_op jit(solution)/shard_map/dot_general | solution.py:82
  99.8 3.6 %collective-permute-start.6 = (bf16[64,384]{1,0:T(8,128)(2,1)}, bf16[64,384]{1,0:T(8,128)(2,1)}, u32[]{:S(2)}, u32[]{:S(2)}) collective-permute-start(bf16[64,384]{1,0:T(8,128)(2,1)} %get-tuple-element.14), channel_id=1, source_target_pairs={{2,0},{4,2},{6,4},{8,6},{10,8},{12,10},{14,12},{3,1},{5,3},{7,5},{... | collective-permute-start | bytes 147464 | tf_op jit(solution)/shard_map/ppermute | solution.py:18
  103.3 3.4 %collective-permute-start.7 = (bf16[64,384]{1,0:T(8,128)(2,1)}, bf16[64,384]{1,0:T(8,128)(2,1)}, u32[]{:S(2)}, u32[]{:S(2)}) collective-permute-start(bf16[64,384]{1,0:T(8,128)(2,1)} %get-tuple-element.15), channel_id=1, source_target_pairs={{0,2},{2,4},{4,6},{6,8},{8,10},{10,12},{12,14},{1,3},{3,5},{5,7},{... | collective-permute-start | bytes 147464 | tf_op jit(solution)/shard_map/ppermute | solution.py:15
  109.5 5.1 %reshape.101 = f32[256,2,1536]{2,1,0:T(2,128)} reshape(f32[512,1536]{1,0:T(8,128)} %convolution_add_fusion.2) | data formatting | bytes 6291456 | tf_op jit(solution)/shard_map/reshape | solution.py:131
  114.5 6.8 %reduce_sum.48 = f32[256,1536]{1,0:T(8,128)} reduce(f32[256,2,1536]{2,1,0:T(2,128)} %reshape.101, f32[]{:T(128)} %constant.15.clone.1), dimensions={1}, to_apply=%region_2.0 | reduce | flops 393216 | bytes 4718596 | tf_op jit(solution)/shard_map/reduce_sum | solution.py:131
  126.0 5.3 %all-to-all-start = ((bf16[8,192,256]{2,1,0:T(8,128)(2,1)}), bf16[8,192,256]{2,1,0:T(8,128)(2,1)}, u32[]{:S(2)}, u32[]{:S(2)}) async-start(bf16[8,192,256]{2,1,0:T(8,128)(2,1)} %bitcast.75), calls=%async_computation | async-start | bytes 1572864 | tf_op jit(solution)/shard_map/all_to_all | solution.py:133
  133.9 5.7 %multiply_reduce_fusion.1 = (f32[512]{0:T(512)S(1)}, f32[512,1536]{1,0:T(8,128)S(1)}) fusion(f32[512,1536]{1,0:T(8,128)S(1)} %copy-done.2, f32[1536]{0:T(1024)S(1)} %get-tuple-element.2, f32[512]{0:T(512)S(1)} %copy-done.23, f32[512,1536]{1,0:T(8,128)S(1)} %fusion.55, f32[512,1536]{1,0:T(8,128)} %fusion.53, bf16[1536,3,384]{2,0,1:T(8,128)(2,1)} %bitcast.86, ...), kind=kOutput, calls=%fused_computation.32 | convolution fusion | flops 625212928 | bytes 14215168 | tf_op jit(solution)/shard_map/dot_general | solution.py:82
  142.5 3.4 %collective-permute-start.9 = (bf16[32,384]{1,0:T(8,128)(2,1)S(1)}, bf16[32,384]{1,0:T(8,128)(2,1)S(1)}, u32[]{:S(2)}, u32[]{:S(2)}) collective-permute-start(bf16[32,384]{1,0:T(8,128)(2,1)S(1)} %get-tuple-element.13), channel_id=1, source_target_pairs={{0,2},{2,4},{4,6},{6,8},{8,10},{10,12},{12,14},{1,3},{3,5},{5,7},{... | collective-permute-start | bytes 73736 | tf_op jit(solution)/shard_map/ppermute | solution.py:15
  153.5 3.2 %multiply_reduce_fusion = (f32[512]{0:T(512)S(1)}, f32[512,1536]{1,0:T(8,128)S(1)}) fusion(f32[512,1536]{1,0:T(8,128)S(1)} %get-tuple-element.36, f32[1536]{0:T(1024)S(1)} %get-tuple-element.3, f32[512]{0:T(512)S(1)} %copy-done.21, f32[512,1536]{1,0:T(8,128)S(1)} %fusion.52, f32[512,1536]{1,0:T(8,128)S(1)} %fusion.50, ...), kind=kOutput, calls=%fused_computation.30 | convolution fusion | flops 625212928 | bytes 14192640 | tf_op jit(solution)/shard_map/dot_general | solution.py:82
  161.7 3.4 %collective-permute-start.11 = (bf16[60,7]{1,0:T(8,128)(2,1)S(1)}, bf16[60,7]{1,0:T(8,128)(2,1)S(1)}, u32[]{:S(2)}, u32[]{:S(2)}) collective-permute-start(bf16[60,7]{1,0:T(8,128)(2,1)S(1)} %get-tuple-element.32), channel_id=1, source_target_pairs={{2,0},{4,2},{6,4},{8,6},{10,8},{12,10},{14,12},{3,1},{5,3},{7,5},{... | collective-permute-start | bytes 2528 | tf_op jit(solution)/shard_map/ppermute | solution.py:18
  165.1 3.1 %collective-permute-done.11 = bf16[60,7]{1,0:T(8,128)(2,1)S(1)} collective-permute-done((bf16[60,7]{1,0:T(8,128)(2,1)S(1)}, bf16[60,7]{1,0:T(8,128)(2,1)S(1)}, u32[]{:S(2)}, u32[]{:S(2)}) %collective-permute-start.11) | collective-permute-done | bytes 872 | tf_op jit(solution)/shard_map/ppermute | solution.py:18
  (129 shorter events, 63.9 us)
Async XLA Ops:
  7.2 51.5 %all-gather.9.cloned.1.call-start = ((), (), s32[]{:S(2)}) async-start(), calls=%async_computation.2 | async-start | bytes 5308416 | tf_op jit(solution)/shard_map/all_gather | solution.py:93
  11.4 54.4 %all-gather.11.cloned.1.call-start = ((), (), s32[]{:S(2)}) async-start(), calls=%async_computation.3 | async-start | bytes 1769472 | tf_op jit(solution)/shard_map/all_gather | solution.py:94
  12.7 66.9 %all-gather.13.cloned.1.call-start = ((), (), s32[]{:S(2)}) async-start(), calls=%async_computation.4 | async-start | bytes 5308416 | tf_op jit(solution)/shard_map/all_gather | solution.py:93
  12.7 14.7 %copy-start.28 = (f32[2,1536]{1,0:T(2,128)S(1)}, f32[2,1536]{1,0:T(2,128)}, u32[]{:S(2)}) copy-start(f32[2,1536]{1,0:T(2,128)} %param.8) | copy-start | bytes 36868
  12.7 14.7 %copy-start.19 = (bf16[15,4,1536]{2,1,0:T(4,128)(2,1)S(1)}, bf16[15,4,1536]{2,1,0:T(4,128)(2,1)}, u32[]{:S(2)}) copy-start(bf16[15,4,1536]{2,1,0:T(4,128)(2,1)} %param.7) | copy-start | bytes 552964
  13.5 14.0 %collective-permute-start = (s32[7]{0:T(128)S(1)}, s32[7]{0:T(128)S(1)}, u32[]{:S(2)}, u32[]{:S(2)}) collective-permute-start(s32[7]{0:T(128)S(1)} %get-tuple-element.33), channel_id=1, source_target_pairs={{0,2},{2,4},{4,6},{6,8},{8,10},{10,12},{12,14},{1,3},{3,5},{5,7},{... | collective-permute-start | bytes 92 | tf_op jit(solution)/shard_map/ppermute | solution.py:15
  17.0 10.6 %collective-permute-start.1 = (s32[7]{0:T(128)S(1)}, s32[7]{0:T(128)S(1)}, u32[]{:S(2)}, u32[]{:S(2)}) collective-permute-start(s32[7]{0:T(128)S(1)} %get-tuple-element.34), channel_id=1, source_target_pairs={{2,0},{4,2},{6,4},{8,6},{10,8},{12,10},{14,12},{3,1},{5,3},{7,5},{... | collective-permute-start | bytes 92 | tf_op jit(solution)/shard_map/ppermute | solution.py:18
  20.6 22.7 %all-to-all-start.1 = ((bf16[192,8,256]{2,0,1:T(8,128)(2,1)}), bf16[192,8,256]{2,0,1:T(8,128)(2,1)}, u32[]{:S(2)}, u32[]{:S(2)}) async-start(bf16[192,8,256]{2,0,1:T(8,128)(2,1)} %copy.14), calls=%async_computation.1 | async-start | bytes 1572864 | tf_op jit(solution)/shard_map/all_to_all | solution.py:134
  26.8 64.2 %all-gather.15.cloned.1.call-start = ((), (), s32[]{:S(2)}) async-start(), calls=%async_computation.5 | async-start | bytes 1769472 | tf_op jit(solution)/shard_map/all_gather | solution.py:94
  29.7 16.1 %copy-start.24 = (f32[512]{0:T(512)}, f32[512]{0:T(512)S(1)}, u32[]{:S(2)}) copy-start(f32[512]{0:T(512)S(1)} %get-tuple-element.35) | copy-start | bytes 6148
  32.7 31.2 %collective-permute-start.2 = (bf16[32,1536]{1,0:T(8,128)(2,1)S(1)}, bf16[32,1536]{1,0:T(8,128)(2,1)S(1)}, u32[]{:S(2)}, u32[]{:S(2)}) collective-permute-start(bf16[32,1536]{1,0:T(8,128)(2,1)S(1)} %get-tuple-element.8), channel_id=1, source_target_pairs={{0,2},{2,4},{4,6},{6,8},{8,10},{10,12},{12,14},{1,3},{3,5},{5,7},{... | collective-permute-start | bytes 294920 | tf_op jit(solution)/shard_map/ppermute | solution.py:15
  36.1 25.4 %collective-permute-start.3 = (bf16[32,1536]{1,0:T(8,128)(2,1)S(1)}, bf16[32,1536]{1,0:T(8,128)(2,1)}, u32[]{:S(2)}, u32[]{:S(2)}) collective-permute-start(bf16[32,1536]{1,0:T(8,128)(2,1)S(1)} %get-tuple-element.9), channel_id=1, source_target_pairs={{2,0},{4,2},{6,4},{8,6},{10,8},{12,10},{14,12},{3,1},{5,3},{7,5},{... | collective-permute-start | bytes 294920 | tf_op jit(solution)/shard_map/ppermute | solution.py:18
  72.8 15.4 %collective-permute-start.4 = (bf16[64,1536]{1,0:T(8,128)(2,1)S(1)}, bf16[64,1536]{1,0:T(8,128)(2,1)}, u32[]{:S(2)}, u32[]{:S(2)}) collective-permute-start(bf16[64,1536]{1,0:T(8,128)(2,1)S(1)} %get-tuple-element.6), channel_id=1, source_target_pairs={{0,2},{2,4},{4,6},{6,8},{8,10},{10,12},{12,14},{1,3},{3,5},{5,7},{... | collective-permute-start | bytes 589832 | tf_op jit(solution)/shard_map/ppermute | solution.py:15
  77.7 8.6 %collective-permute-start.5 = (bf16[64,1536]{1,0:T(8,128)(2,1)S(1)}, bf16[64,1536]{1,0:T(8,128)(2,1)}, u32[]{:S(2)}, u32[]{:S(2)}) collective-permute-start(bf16[64,1536]{1,0:T(8,128)(2,1)S(1)} %get-tuple-element.7), channel_id=1, source_target_pairs={{2,0},{4,2},{6,4},{8,6},{10,8},{12,10},{14,12},{3,1},{5,3},{7,5},{... | collective-permute-start | bytes 589832 | tf_op jit(solution)/shard_map/ppermute | solution.py:18
  91.0 15.7 %copy-start.18 = (f32[512,384]{1,0:T(8,128)S(1)}, f32[512,384]{1,0:T(8,128)}, u32[]{:S(2)}) copy-start(f32[512,384]{1,0:T(8,128)} %fusion.39) | copy-start | bytes 2359300
  94.8 11.9 %copy-start.1 = (f32[512,1536]{1,0:T(8,128)S(1)}, f32[512,1536]{1,0:T(8,128)}, u32[]{:S(2)}) copy-start(f32[512,1536]{1,0:T(8,128)} %copy-done) | copy-start | bytes 9437188
  94.8 11.9 %copy-start.15 = (bf16[1,1536,384]{2,1,0:T(8,128)(2,1)S(1)}, bf16[1,1536,384]{2,1,0:T(8,128)(2,1)}, u32[]{:S(2)}) copy-start(bf16[1,1536,384]{2,1,0:T(8,128)(2,1)} %all-gather.15.cloned.1.call-done) | copy-start | bytes 3538948
  99.8 34.1 %collective-permute-start.6 = (bf16[64,384]{1,0:T(8,128)(2,1)}, bf16[64,384]{1,0:T(8,128)(2,1)}, u32[]{:S(2)}, u32[]{:S(2)}) collective-permute-start(bf16[64,384]{1,0:T(8,128)(2,1)} %get-tuple-element.14), channel_id=1, source_target_pairs={{2,0},{4,2},{6,4},{8,6},{10,8},{12,10},{14,12},{3,1},{5,3},{7,5},{... | collective-permute-start | bytes 147464 | tf_op jit(solution)/shard_map/ppermute | solution.py:18
  103.3 28.0 %collective-permute-start.7 = (bf16[64,384]{1,0:T(8,128)(2,1)}, bf16[64,384]{1,0:T(8,128)(2,1)}, u32[]{:S(2)}, u32[]{:S(2)}) collective-permute-start(bf16[64,384]{1,0:T(8,128)(2,1)} %get-tuple-element.15), channel_id=1, source_target_pairs={{0,2},{2,4},{4,6},{6,8},{8,10},{10,12},{12,14},{1,3},{3,5},{5,7},{... | collective-permute-start | bytes 147464 | tf_op jit(solution)/shard_map/ppermute | solution.py:15
  126.0 42.9 %all-to-all-start = ((bf16[8,192,256]{2,1,0:T(8,128)(2,1)}), bf16[8,192,256]{2,1,0:T(8,128)(2,1)}, u32[]{:S(2)}, u32[]{:S(2)}) async-start(bf16[8,192,256]{2,1,0:T(8,128)(2,1)} %bitcast.75), calls=%async_computation | async-start | bytes 1572864 | tf_op jit(solution)/shard_map/all_to_all | solution.py:133
  142.5 7.2 %collective-permute-start.9 = (bf16[32,384]{1,0:T(8,128)(2,1)S(1)}, bf16[32,384]{1,0:T(8,128)(2,1)S(1)}, u32[]{:S(2)}, u32[]{:S(2)}) collective-permute-start(bf16[32,384]{1,0:T(8,128)(2,1)S(1)} %get-tuple-element.13), channel_id=1, source_target_pairs={{0,2},{2,4},{4,6},{6,8},{8,10},{10,12},{12,14},{1,3},{3,5},{5,7},{... | collective-permute-start | bytes 73736 | tf_op jit(solution)/shard_map/ppermute | solution.py:15
  146.9 6.6 %collective-permute-start.8 = (bf16[32,384]{1,0:T(8,128)(2,1)S(1)}, bf16[32,384]{1,0:T(8,128)(2,1)S(1)}, u32[]{:S(2)}, u32[]{:S(2)}) collective-permute-start(bf16[32,384]{1,0:T(8,128)(2,1)S(1)} %get-tuple-element.12), channel_id=1, source_target_pairs={{2,0},{4,2},{6,4},{8,6},{10,8},{12,10},{14,12},{3,1},{5,3},{7,5},{... | collective-permute-start | bytes 73736 | tf_op jit(solution)/shard_map/ppermute | solution.py:18
  159.2 5.9 %collective-permute-start.10 = (bf16[60,7]{1,0:T(8,128)(2,1)S(1)}, bf16[60,7]{1,0:T(8,128)(2,1)S(1)}, u32[]{:S(2)}, u32[]{:S(2)}) collective-permute-start(bf16[60,7]{1,0:T(8,128)(2,1)S(1)} %get-tuple-element.31), channel_id=1, source_target_pairs={{0,2},{2,4},{4,6},{6,8},{8,10},{10,12},{12,14},{1,3},{3,5},{5,7},{... | collective-permute-start | bytes 2528 | tf_op jit(solution)/shard_map/ppermute | solution.py:15
  161.7 6.5 %collective-permute-start.11 = (bf16[60,7]{1,0:T(8,128)(2,1)S(1)}, bf16[60,7]{1,0:T(8,128)(2,1)S(1)}, u32[]{:S(2)}, u32[]{:S(2)}) collective-permute-start(bf16[60,7]{1,0:T(8,128)(2,1)S(1)} %get-tuple-element.32), channel_id=1, source_target_pairs={{2,0},{4,2},{6,4},{8,6},{10,8},{12,10},{14,12},{3,1},{5,3},{7,5},{... | collective-permute-start | bytes 2528 | tf_op jit(solution)/shard_map/ppermute | solution.py:18
  (24 other events, 86.9 us)
Sparse Core Ops, SparseCore 0:
  11.6 14.0 all-gather.8
  27.2 10.3 all-gather.10
  39.2 13.8 all-gather.12
  54.5 10.3 all-gather.14
where the time goes:
time: 181 us; the launch traced here: 178 us
  starting transfers between devices  49.3 us (27%)
  matrix products  45.4 us (25%)
  local copies, waits for them, and re-layouts  37.8 us (21%)
  other arithmetic  16 us (9%)
  waiting for transfers between devices  15.4 us (9%)
  between operations  14.4 us (8%)
    ppermute x6, starting transfers between devices, with_halo(): lax.ppermute(lax.slice_in_dim(block, block.shape[dim] - width, None, axis...  20.9 us
    dot_general x6, matrix products, taps_backward(): lax.dot_general(window, convolution_result[:, tap_index, :], (((1,), (1,)...  17.7 us
    ppermute x6, starting transfers between devices, with_halo(): lax.ppermute(lax.slice_in_dim(block, 0, width, axis=dim), axis, backward)  16.7 us
    dot_general x6, matrix products, taps_forward(): jnp.dot(window, convolution_result[:, tap_index, :], preferred_element_ty...  14.2 us
    ppermute x6, waiting for transfers between devices, with_halo(): lax.ppermute(lax.slice_in_dim(block, 0, width, axis=dim), axis, backward)  9.67 us
    reduce_sum x1, other arithmetic, body(): jnp.mean(hidden.reshape(shard_local_rows // POOL, POOL, hidden.shape[1]),...  6.78 us
    unnamed x61, local copies, waits for them, and re-layouts  6.25 us
    all_to_all x1, starting transfers between devices, body(): lax.all_to_all(cotangent[0], 'seq', split_axis=1, concat_axis=0, tiled=True)  6.22 us
  transfers between devices with their start and end apart: 18, of which 4 were waited for; matrix products, arithmetic and copies ran while one was open for 43% of the time, Pallas kernels for 0%

commit v1 on v0

v1 whole, which is shorter than its diff:
```python
import functools

import jax
import jax.numpy as jnp
from jax import lax
from jax.experimental import pallas as pl
from jax.experimental.pallas import tpu as pltpu
from jax.sharding import PartitionSpec as P

D0 = 32
D1 = 64
POOL = 2
EDGE = 128
GC = 0.7978845608028654
GA = 0.044715
F32 = jnp.float32
BF16 = jnp.bfloat16
MESH = pl.DeviceIdType.MESH


def nn(a, b):
    return lax.dot_general(a, b, (((1,), (0,)), ((), ())), preferred_element_type=F32)


def nt(a, b):
    return lax.dot_general(a, b, (((1,), (1,)), ((), ())), preferred_element_type=F32)


def gelu(x):
    return (0.5 * x) * (1.0 + jnp.tanh(x * (GC + (GC * GA) * (x * x))))


def gelu_slope(x):
    xx = x * x
    t = jnp.tanh(x * (GC + (GC * GA) * xx))
    return 0.5 * (1.0 + t) + (0.5 * x) * (1.0 - t * t) * (GC + (3.0 * GC * GA) * xx)


def kernel(n, codes, stem, gains, wconv, wpoint, cot, pooled_out, sal_out,
           wc, wp, oh, h0, act0, co0, h1, act1, co1, pool, sendp, recc, cott, grad, ga,
           gc1, gc0, glo, code_l, code_r, pj_l, pj_r, pj_s,
           wl_sem, ws_sem, wr_sem, cs_sem, cr_sem, ps_sem, pr_sem, own_sem,
           hs_sem, hr_sem):
    me = lax.axis_index("seq")
    f = lax.axis_index("fsdp")
    rows = codes.shape[1]
    ch = cot.shape[1]
    half = wpoint.shape[1]
    chan = 2 * half
    prow = rows // POOL
    layers = wpoint.shape[0]
    left, right = me - 1, me + 1
    has_left, has_right = me > 0, me < n - 1
    e0 = D0 + D1

    def local_w():
        copies = []
        for l in range(layers):
            copies.append(pltpu.make_async_copy(wconv.at[l], wc.at[l, :, pl.ds(pl.multiple_of(f * half, half), half), :], wl_sem.at[2 * l]))
            copies.append(pltpu.make_async_copy(wpoint.at[l], wp.at[l, pl.ds(pl.multiple_of(f * half, half), half), :], wl_sem.at[2 * l + 1]))
        return copies

    def remote_w():
        copies = []
        for l in range(layers):
            copies.append(pltpu.make_async_remote_copy(
                wconv.at[l], wc.at[l, :, pl.ds(pl.multiple_of(f * half, half), half), :],
                ws_sem.at[2 * l], wr_sem.at[2 * l], device_id={"fsdp": 1 - f}, device_id_type=MESH))
            copies.append(pltpu.make_async_remote_copy(
                wpoint.at[l], wp.at[l, pl.ds(pl.multiple_of(f * half, half), half), :],
                ws_sem.at[2 * l + 1], wr_sem.at[2 * l + 1], device_id={"fsdp": 1 - f}, device_id_type=MESH))
        return copies

    own_w, sib_w = local_w(), remote_w()
    for c in own_w:
        c.start()

    barrier = pltpu.get_barrier_semaphore()

    @pl.loop(1, n)
    def _(i):
        pl.semaphore_signal(barrier, inc=1, device_id={"seq": lax.rem(me + i, n)}, device_id_type=MESH)

    pl.semaphore_signal(barrier, inc=1, device_id={"fsdp": 1 - f}, device_id_type=MESH)
    pl.semaphore_wait(barrier, n)

    def edge(k, to_left_src, to_left_dst, to_right_src, to_right_dst):
        tl = pltpu.make_async_remote_copy(to_left_src, to_left_dst, hs_sem.at[2 * k], hr_sem.at[2 * k],
                                          device_id={"seq": left}, device_id_type=MESH)
        tr = pltpu.make_async_remote_copy(to_right_src, to_right_dst, hs_sem.at[2 * k + 1], hr_sem.at[2 * k + 1],
                                          device_id={"seq": right}, device_id_type=MESH)

        def start():
            pl.when(has_left)(lambda: tl.start())
            pl.when(has_right)(lambda: tr.start())

        def recv():
            pl.when(has_right)(lambda: tl.wait_recv())
            pl.when(has_left)(lambda: tr.wait_recv())

        def sent():
            pl.when(has_left)(lambda: tl.wait_send())
            pl.when(has_right)(lambda: tr.wait_send())

        return start, recv, sent

    codes_x = edge(0, codes.at[:, pl.ds(0, EDGE)], code_r, codes.at[:, pl.ds(rows - EDGE, EDGE)], code_l)
    codes_x[0]()
    sib_w[0].start()
    sib_w[1].start()

    def cot_copy(i, slot):
        peer = lax.rem(me + i, n)
        return pltpu.make_async_remote_copy(
            cot.at[0, :, pl.ds(pl.multiple_of(peer * prow, 128), prow)], recc.at[slot],
            cs_sem.at[i], cr_sem.at[i], device_id={"seq": peer}, device_id_type=MESH)

    cot_own = pltpu.make_async_copy(cot.at[0, :, pl.ds(pl.multiple_of(me * prow, 128), prow)], recc.at[me], own_sem.at[0])
    cot_own.start()

    @pl.loop(1, n)
    def _(i):
        cot_copy(i, me).start()

    sib_w[2].start()
    sib_w[3].start()

    @pl.when(jnp.logical_not(has_left))
    def _():
        code_l[...] = jnp.full(code_l.shape, -1, jnp.int32)
        gc1[pl.ds(0, D1), :] = jnp.zeros((D1, gc1.shape[1]), BF16)
        gc0[pl.ds(0, D0), :] = jnp.zeros((D0, gc0.shape[1]), BF16)
        pj_l[...] = jnp.zeros(pj_l.shape, BF16)

    @pl.when(jnp.logical_not(has_right))
    def _():
        code_r[...] = jnp.full(code_r.shape, -1, jnp.int32)
        gc1[pl.ds(D1 + rows, D1), :] = jnp.zeros((D1, gc1.shape[1]), BF16)
        gc0[pl.ds(D0 + rows, D0), :] = jnp.zeros((D0, gc0.shape[1]), BF16)
        pj_r[...] = jnp.zeros(pj_r.shape, BF16)

    codes_x[1]()

    wide = rows + 2 * EDGE
    ext = jnp.concatenate([code_l[...], codes[...], code_r[...]], axis=1)
    ext = jnp.broadcast_to(ext, (8, wide))
    sub = lax.broadcasted_iota(jnp.int32, (8, wide), 0)
    low_half = sub < 4
    base = jnp.where(low_half, sub, sub - 4)
    groups = []
    off = EDGE - e0 - 7
    for j in range(8):
        a = pltpu.roll(ext, wide - (off + 2 * j), 1)
        b = pltpu.roll(ext, wide - (off + 2 * j + 1), 1)
        groups.append(jnp.where(jnp.where(low_half, a, b) == base, 1.0, 0.0).astype(F32))
    oh[...] = jnp.concatenate(groups, axis=0).T.astype(BF16)

    ext0 = rows + 2 * e0
    hb = ext0 // 4

    @pl.loop(0, 4)
    def _(b):
        s = pl.multiple_of(b * hb, 16)
        h0[pl.ds(s, hb), :] = nn(oh[pl.ds(s, hb), :], stem[...])

    def activate(src, dst, count, halo, layer):
        gain = gains[pl.ds(layer, 1), :]

        @pl.loop(0, count // 16, unroll=2)
        def _(b):
            s = pl.multiple_of(b * 16, 16)
            x = src[pl.ds(s, 16), :]
            r = lax.rsqrt(jnp.sum(x * x, axis=1, keepdims=True) * (1.0 / chan) + 1e-06)
            pos = me * rows - halo + s + lax.broadcasted_iota(jnp.int32, (16, 1), 0)
            keep = jnp.where((pos >= 0) & (pos < n * rows), 1.0, 0.0)
            dst[pl.ds(s, 16), :] = (gelu(x * r * gain) * keep).astype(BF16)

    activate(h0, act0, ext0, e0, 0)

    own_w[0].wait()
    sib_w[0].wait_recv()
    own_w[1].wait()
    sib_w[1].wait_recv()

    def taps(ref, start, count, d, order):
        return jnp.concatenate([ref[pl.ds(pl.multiple_of(start + k * d, 32), count), :] for k in order], axis=1)

    ext1 = rows + 2 * D1
    b1 = ext1 // 2
    flat = (3 * chan, wc.shape[3])

    @pl.loop(0, 2)
    def _(b):
        s = pl.multiple_of(b * b1, 64)
        c = nn(taps(act0, s, b1, D0, (0, 1, 2)), wc[0].reshape(flat))
        co0[pl.ds(s, b1), :] = c
        h1[pl.ds(s, b1), :] = h0[pl.ds(pl.multiple_of(s + D0, 32), b1), :] + nt(gelu(c).astype(BF16), wp[0])

    activate(h1, act1, ext1, D1, 1)

    own_w[2].wait()
    sib_w[2].wait_recv()
    own_w[3].wait()
    sib_w[3].wait_recv()

    b2 = rows // 2
    pb = b2 // POOL
    pr = lax.broadcasted_iota(jnp.int32, (pb, b2), 0)
    pc = lax.broadcasted_iota(jnp.int32, (pb, b2), 1)
    pool_mat = jnp.where((pc == 2 * pr) | (pc == 2 * pr + 1), 0.5, 0.0).astype(BF16)

    @pl.loop(0, 2)
    def _(b):
        s = pl.multiple_of(b * b2, 64)
        c = nn(taps(act1, s, b2, D1, (0, 1, 2)), wc[1].reshape(flat))
        co1[pl.ds(s, b2), :] = c
        h2 = h1[pl.ds(pl.multiple_of(s + D1, 64), b2), :] + nt(gelu(c).astype(BF16), wp[1])
        hi = h2.astype(BF16)
        lo = (h2 - hi.astype(F32)).astype(BF16)
        pool[pl.ds(pl.multiple_of(b * pb, 64), pb), :] = nn(pool_mat, hi) + nn(pool_mat, lo)

    sendp[...] = pool[...].T.reshape(n, ch, prow).astype(BF16)

    def pool_copy(i, slot):
        peer = lax.rem(me + i, n)
        return pltpu.make_async_remote_copy(
            sendp.at[peer], pooled_out.at[0, :, pl.ds(pl.multiple_of(slot * prow, 128), prow)],
            ps_sem.at[i], pr_sem.at[i], device_id={"seq": peer}, device_id_type=MESH)

    pool_own = pltpu.make_async_copy(sendp.at[me], pooled_out.at[0, :, pl.ds(pl.multiple_of(me * prow, 128), prow)], own_sem.at[1])
    pool_own.start()

    @pl.loop(1, n)
    def _(i):
        pool_copy(i, me).start()

    cot_own.wait()

    @pl.loop(1, n)
    def _(i):
        cot_copy(i, lax.rem(me + n - i, n)).wait_recv()

    cott[...] = recc[...].astype(F32).reshape(chan, prow).astype(BF16)
    er = lax.broadcasted_iota(jnp.int32, (b2, pb), 0)
    ec = lax.broadcasted_iota(jnp.int32, (b2, pb), 1)
    spread = jnp.where((er == 2 * ec) | (er == 2 * ec + 1), 0.5, 0.0).astype(BF16)

    @pl.loop(0, 2)
    def _(b):
        s = pl.multiple_of(b * b2, 64)
        g = nt(spread, cott[:, pl.ds(pl.multiple_of(b * pb, 128), pb)])
        grad[pl.ds(s, b2), :] = g
        gb = nn(g.astype(BF16), wp[1])
        gc1[pl.ds(pl.multiple_of(D1 + s, 64), b2), :] = (gb * gelu_slope(co1[pl.ds(s, b2), :])).astype(BF16)

    def back(x_edge, gc, d, layer, hidden, hoff, low):
        gain = gains[pl.ds(layer, 1), :]
        x_edge[1]()

        @pl.loop(0, 2)
        def _(b):
            s = pl.multiple_of(b * b2, 64)
            w = jnp.concatenate([wc[layer, 0], wc[layer, 1], wc[layer, 2]], axis=1)
            ga[pl.ds(s, b2), :] = nt(taps(gc, s, b2, d, (2, 1, 0)), w)

        @pl.loop(0, rows // 16, unroll=2)
        def _(b):
            s = pl.multiple_of(b * 16, 16)
            x = hidden[pl.ds(pl.multiple_of(s + hoff, 16), 16), :]
            r = lax.rsqrt(jnp.sum(x * x, axis=1, keepdims=True) * (1.0 / chan) + 1e-06)
            dn = ga[pl.ds(s, 16), :] * gelu_slope(x * r * gain) * gain
            m = jnp.sum(dn * x, axis=1, keepdims=True) * (r * r * r * (1.0 / chan))
            g = grad[pl.ds(s, 16), :] + (dn * r - x * m)
            if low is None:
                grad[pl.ds(s, 16), :] = g
            else:
                hi = g.astype(BF16)
                low[0, pl.ds(s, 16), :] = hi
                low[1, pl.ds(s, 16), :] = (g - hi.astype(F32)).astype(BF16)

    x1 = edge(1, gc1.at[pl.ds(D1, D1), :], gc1.at[pl.ds(D1 + rows, D1), :],
              gc1.at[pl.ds(rows, D1), :], gc1.at[pl.ds(0, D1), :])
    x1[0]()
    back(x1, gc1, D1, 1, h1, D1, None)

    @pl.loop(0, 2)
    def _(b):
        s = pl.multiple_of(b * b2, 64)
        gb = nn(grad[pl.ds(s, b2), :].astype(BF16), wp[0])
        gc0[pl.ds(pl.multiple_of(D0 + s, 32), b2), :] = (gb * gelu_slope(co0[pl.ds(pl.multiple_of(s + D1, 64), b2), :])).astype(BF16)

    x0 = edge(2, gc0.at[pl.ds(D0, D0), :], gc0.at[pl.ds(D0 + rows, D0), :],
              gc0.at[pl.ds(rows, D0), :], gc0.at[pl.ds(0, D0), :])
    x0[0]()
    back(x0, gc0, D0, 0, h0, e0, glo)

    proj = nt(stem[...], glo[0]) + nt(stem[...], glo[1])
    pj_s[0] = proj[:, 0:EDGE].astype(BF16)
    pj_s[1] = proj[:, rows - EDGE:rows].astype(BF16)
    xp = edge(3, pj_s.at[0], pj_r, pj_s.at[1], pj_l)
    xp[0]()
    xp[1]()
    full = jnp.concatenate([pj_l[...].astype(F32), proj, pj_r[...].astype(F32)], axis=1)
    total = jnp.zeros((8, wide), F32)
    for j in range(8):
        grp = full[8 * j:8 * j + 8, :]
        a = pltpu.roll(grp, (2 * j - 7) % wide, 1)
        b = pltpu.roll(grp, (2 * j - 6) % wide, 1)
        total = total + jnp.where(low_half, a, b)
    both = total + pltpu.roll(total, 4, 0)
    sal_out[0] = both[0:4, EDGE:EDGE + rows]

    pool_own.wait()

    @pl.loop(1, n)
    def _(i):
        cot_copy(i, me).wait_send()
        pool_copy(i, lax.rem(me + n - i, n)).wait_recv()
        pool_copy(i, me).wait_send()

    for c in sib_w:
        c.wait_send()
    for x in (codes_x, x1, x0, xp):
        x[2]()


def body(n, base_codes, stem_weight, norm_gains, conv_weight, point_weight, cotangent):
    rows = base_codes.shape[1]
    ch, prow = cotangent.shape[1], rows // POOL
    layers, half, taps_n, ff = conv_weight.shape
    chan = 2 * half
    taps_b = stem_weight.shape[0] * stem_weight.shape[1]
    stem = jnp.pad(stem_weight.reshape(taps_b, chan), ((0, 64 - taps_b), (0, 0)))
    wconv = conv_weight.transpose(0, 2, 1, 3)
    any_spec = pl.BlockSpec(memory_space=pl.ANY)
    vm = pl.BlockSpec(memory_space=pltpu.VMEM)
    ext0, ext1 = rows + 2 * (D0 + D1), rows + 2 * D1
    V = pltpu.VMEM
    DMA = pltpu.SemaphoreType.DMA
    return pl.pallas_call(
        functools.partial(kernel, n),
        out_shape=(jax.ShapeDtypeStruct(cotangent.shape, BF16),
                   jax.ShapeDtypeStruct((1, 4, rows), F32)),
        in_specs=[vm, vm, vm, any_spec, any_spec, any_spec],
        out_specs=(any_spec, vm),
        scratch_shapes=[
            V((layers, taps_n, chan, ff), BF16), V((layers, chan, ff), BF16),
            V((rows + 2 * EDGE, 64), BF16),
            V((ext0, chan), F32), V((ext0, chan), BF16), V((ext1, ff), F32),
            V((ext1, chan), F32), V((ext1, chan), BF16), V((rows, ff), F32),
            V((prow, chan), F32), V((n, ch, prow), BF16), V((n, ch, prow), BF16),
            V((chan, prow), BF16), V((rows, chan), F32), V((rows, chan), F32),
            V((ext1, ff), BF16), V((rows + 2 * D0, ff), BF16), V((2, rows, chan), BF16),
            V((1, EDGE), jnp.int32), V((1, EDGE), jnp.int32),
            V((64, EDGE), BF16), V((64, EDGE), BF16), V((2, 64, EDGE), BF16),
            DMA((2 * layers,)), DMA((2 * layers,)), DMA((2 * layers,)),
            DMA((n,)), DMA((n,)), DMA((n,)), DMA((n,)), DMA((2,)),
            DMA((8,)), DMA((8,)),
        ],
        compiler_params=pltpu.CompilerParams(
            collective_id=0, has_side_effects=True, vmem_limit_bytes=56 * 1024 * 1024),
        cost_estimate=pl.CostEstimate(flops=10_000_000_000, bytes_accessed=12_000_000, transcendentals=4_000_000),
    )(base_codes, stem, norm_gains, wconv, point_weight, cotangent)


def solution(mesh):
    in_specs = (
        P(("grp", "fsdp"), "seq"),
        P(),
        P(),
        P(None, "fsdp", None, None),
        P(None, "fsdp", None),
        P(("grp", "fsdp"), "seq", None),
    )
    out_specs = (P(("grp", "fsdp"), "seq", None), P(("grp", "fsdp"), None, "seq"))
    return jax.shard_map(functools.partial(body, mesh.shape["seq"]), mesh=mesh,
                         in_specs=in_specs, out_specs=out_specs, check_vma=False)
```

time: 181 us -> 75.2 us (0.42); the launches traced: 178 us -> 74.9 us
  Pallas kernels: 0 us -> 69.2 us
  starting transfers between devices: 49.3 us -> 0 us
  matrix products: 45.4 us -> 0 us
  local copies, waits for them, and re-layouts: 37.8 us -> 5.05 us
  other arithmetic: 16 us -> 0 us
  waiting for transfers between devices: 15.4 us -> 0 us
  between operations: 14.4 us -> 0.64 us
    pallas_call x0 -> x1, Pallas kernels: none -> 69.2 us  [body(): pl.pallas_call(functools.partial(kernel, n), out_shape=(jax.ShapeDtypeStr...]
    dot_general x18 -> x0, matrix products: 45.4 us -> none  [the longest x6 17.7 us: taps_backward(): lax.dot_general(window, convolution_result[:, tap_index, :], (((1,), (1,)...]
    ppermute x12 -> x0, starting transfers between devices: 37.6 us -> none  [the longest x6 20.9 us: with_halo(): lax.ppermute(lax.slice_in_dim(block, block.shape[dim] - width, None, axis...]
    all_to_all x2 -> x0, starting transfers between devices: 11.5 us -> none  [the longest x1 6.22 us: body(): lax.all_to_all(cotangent[0], 'seq', split_axis=1, concat_axis=0, tiled=True)]
    ppermute x12 -> x0, waiting for transfers between devices: 9.69 us -> none  [the longest x6 9.67 us: with_halo(): lax.ppermute(lax.slice_in_dim(block, 0, width, axis=dim), axis, backward)]
    reshape x3 -> x1, local copies, waits for them, and re-layouts: 10.3 us -> 0.97 us  [body(): stem_weight.reshape(taps_b, chan)]
    reduce_sum x1 -> x0, other arithmetic: 6.78 us -> none  [body(): jnp.mean(hidden.reshape(shard_local_rows // POOL, POOL, hidden.shape[1]),...]
    slice x10 -> x0, local copies, waits for them, and re-layouts: 6.59 us -> none  [the longest x1 4.18 us: fetch_panels(): conv_weight[layer_number_index]]
  transfers between devices with their start and end apart: 18 -> 0, of which waited for: 4 -> 0; matrix products, arithmetic and copies ran while one was open for 43% -> 0% of each run, Pallas kernels for 0% -> 0%
where the time goes in v1:
time: 75.2 us; the launch traced here: 74.9 us
  Pallas kernels  69.2 us (92%)
  local copies, waits for them, and re-layouts  5.05 us (7%)
    pallas_call x1, Pallas kernels, body(): pl.pallas_call(functools.partial(kernel, n), out_shape=(jax.ShapeDtypeStr...  69.2 us
    unnamed x2, local copies, waits for them, and re-layouts  3.38 us

profile of v1, /device:TPU:10, one launch (start us, length us, event | category | flops | bytes accessed | tf_op | source)
XLA Modules:
  0.0 74.9 jit_solution(5809021119738397729)
XLA Ops:
  0.6 1.0 %reshape.7 = bf16[60,1536]{1,0:T(8,128)(2,1)S(1)} reshape(bf16[15,4,1536]{2,1,0:T(4,128)(2,1)} %param.7) | data formatting | bytes 368640 | tf_op jit(solution)/shard_map/reshape | solution.py:333
  1.6 0.7 pad.4.stem
  2.3 69.2 %shard_map.77 = (bf16[1,192,2048]{2,1,0:T(8,128)(2,1)}, f32[1,4,512]{2,1,0:T(4,128)}) custom-call(s32[1,512]{1,0:T(1,128)} %codes.1, bf16[64,1536]{1,0:T(8,128)(2,1)} %pad.4.stem, f32[2,1536]{1,0:T(2,128)} %gains.1, bf16[2,3,768,384]{3,2,1,0:T(8,128)(2,1)} %bitcast.1, bf16[2,768,384]{2,1,0:T(8,128)(2,1)} %wpoint.1, bf16[1,192,2048]{2,1,0:T(8,128)(2,1)} %cot.1), custom_call_target="tpu_custom_call" | custom-call | flops 10000000000 | bytes 12000000 | tf_op jit(solution)/shard_map/pallas_call | solution.py:340
  71.5 2.1 %copy.10 = bf16[1,192,2048]{2,1,0:T(8,128)(2,1)} copy(bf16[1,192,2048]{2,1,0:T(8,128)(2,1)} %get-tuple-element.4) | data formatting | bytes 1572864
  73.6 1.3 %copy.11 = f32[1,4,512]{2,1,0:T(4,128)} copy(f32[1,4,512]{2,1,0:T(4,128)} %get-tuple-element.5) | data formatting | bytes 16384

commit v2 on v1

--- a/solution.py
+++ b/solution.py
@@ -36,9 +36,9 @@
     return 0.5 * (1.0 + t) + (0.5 * x) * (1.0 - t * t) * (GC + (3.0 * GC * GA) * xx)
 
 
-def kernel(n, codes, stem, gains, wconv, wpoint, cot, pooled_out, sal_out,
+def kernel(n, codes, stem3, gains, wconv, wpoint, cot, pooled_out, sal_out,
            wc, wp, oh, h0, act0, co0, h1, act1, co1, pool, sendp, recc, cott, grad, ga,
-           gc1, gc0, glo, code_l, code_r, pj_l, pj_r, pj_s,
+           gc1, gc0, glo, code_l, code_r, pj_l, pj_r, pj_s, stem, r0, r1,
            wl_sem, ws_sem, wr_sem, cs_sem, cr_sem, ps_sem, pr_sem, own_sem,
            hs_sem, hr_sem):
     me = lax.axis_index("seq")
@@ -82,6 +82,9 @@
         pl.semaphore_signal(barrier, inc=1, device_id={"seq": lax.rem(me + i, n)}, device_id_type=MESH)
 
     pl.semaphore_signal(barrier, inc=1, device_id={"fsdp": 1 - f}, device_id_type=MESH)
+    for j in range(4):
+        quads = [stem3[k].astype(F32) if k < stem3.shape[0] else jnp.zeros((4, chan), F32) for k in range(4 * j, 4 * j + 4)]
+        stem[pl.ds(16 * j, 16), :] = jnp.concatenate(quads, axis=0).astype(BF16)
     pl.semaphore_wait(barrier, n)
 
     def edge(k, to_left_src, to_left_dst, to_right_src, to_right_dst):
@@ -163,19 +166,20 @@
         s = pl.multiple_of(b * hb, 16)
         h0[pl.ds(s, hb), :] = nn(oh[pl.ds(s, hb), :], stem[...])
 
-    def activate(src, dst, count, halo, layer):
+    def activate(src, dst, scale, count, halo, layer):
         gain = gains[pl.ds(layer, 1), :]
 
         @pl.loop(0, count // 16, unroll=2)
         def _(b):
             s = pl.multiple_of(b * 16, 16)
             x = src[pl.ds(s, 16), :]
-            r = lax.rsqrt(jnp.sum(x * x, axis=1, keepdims=True) * (1.0 / chan) + 1e-06)
             pos = me * rows - halo + s + lax.broadcasted_iota(jnp.int32, (16, 1), 0)
             keep = jnp.where((pos >= 0) & (pos < n * rows), 1.0, 0.0)
-            dst[pl.ds(s, 16), :] = (gelu(x * r * gain) * keep).astype(BF16)
-
-    activate(h0, act0, ext0, e0, 0)
+            r = keep * lax.rsqrt(jnp.sum(x * x, axis=1, keepdims=True) * (1.0 / chan) + 1e-06)
+            scale[pl.ds(s, 16), :] = jnp.broadcast_to(r, (16, 128))
+            dst[pl.ds(s, 16), :] = gelu(x * r * gain).astype(BF16)
+
+    activate(h0, act0, r0, ext0, e0, 0)
 
     own_w[0].wait()
     sib_w[0].wait_recv()
@@ -196,7 +200,7 @@
         co0[pl.ds(s, b1), :] = c
         h1[pl.ds(s, b1), :] = h0[pl.ds(pl.multiple_of(s + D0, 32), b1), :] + nt(gelu(c).astype(BF16), wp[0])
 
-    activate(h1, act1, ext1, D1, 1)
+    activate(h1, act1, r1, ext1, D1, 1)
 
     own_w[2].wait()
     sib_w[2].wait_recv()
@@ -229,10 +233,14 @@
 
     pool_own = pltpu.make_async_copy(sendp.at[me], pooled_out.at[0, :, pl.ds(pl.multiple_of(me * prow, 128), prow)], own_sem.at[1])
     pool_own.start()
-
-    @pl.loop(1, n)
-    def _(i):
-        pool_copy(i, me).start()
+    cut1, cut2 = 1 + (n - 1) // 4, 1 + 5 * (n - 1) // 8
+
+    def pool_send(first, last):
+        @pl.loop(first, last)
+        def _(i):
+            pool_copy(i, me).start()
+
+    pool_send(1, cut1)
 
     cot_own.wait()
 
@@ -241,64 +249,84 @@
         cot_copy(i, lax.rem(me + n - i, n)).wait_recv()
 
     cott[...] = recc[...].astype(F32).reshape(chan, prow).astype(BF16)
-    er = lax.broadcasted_iota(jnp.int32, (b2, pb), 0)
-    ec = lax.broadcasted_iota(jnp.int32, (b2, pb), 1)
-    spread = jnp.where((er == 2 * ec) | (er == 2 * ec + 1), 0.5, 0.0).astype(BF16)
+    er = lax.broadcasted_iota(jnp.int32, (b2, prow), 0)
+    ec = lax.broadcasted_iota(jnp.int32, (b2, prow), 1)
 
     @pl.loop(0, 2)
     def _(b):
         s = pl.multiple_of(b * b2, 64)
-        g = nt(spread, cott[:, pl.ds(pl.multiple_of(b * pb, 128), pb)])
-        grad[pl.ds(s, b2), :] = g
-        gb = nn(g.astype(BF16), wp[1])
-        gc1[pl.ds(pl.multiple_of(D1 + s, 64), b2), :] = (gb * gelu_slope(co1[pl.ds(s, b2), :])).astype(BF16)
-
-    def back(x_edge, gc, d, layer, hidden, hoff, low):
+        row = er + s
+        spread = jnp.where((row == 2 * ec) | (row == 2 * ec + 1), 0.5, 0.0).astype(BF16)
+        grad[pl.ds(s, b2), :] = nt(spread, cott[...])
+
+    q = rows // 4
+    middle, ends = ((q, 2 * q),), ((0, q), (3 * q, q))
+
+    def get(ref, off, part):
+        pieces = [ref[pl.ds(off + s, c), :] for s, c in part]
+        return pieces[0] if len(pieces) == 1 else jnp.concatenate(pieces, axis=0)
+
+    def put(ref, off, part, value):
+        at = 0
+        for s, c in part:
+            ref[pl.ds(off + s, c), :] = value[at:at + c]
+            at += c
+
+    def conv_grad(gc, d, layer, co, coff, part):
+        gb = nn(get(grad, 0, part).astype(BF16), wp[layer])
+        put(gc, d, part, (gb * gelu_slope(get(co, coff, part))).astype(BF16))
+
+    def back(gc, d, layer, hidden, scale, hoff, low, part):
         gain = gains[pl.ds(layer, 1), :]
-        x_edge[1]()
-
-        @pl.loop(0, 2)
-        def _(b):
-            s = pl.multiple_of(b * b2, 64)
-            w = jnp.concatenate([wc[layer, 0], wc[layer, 1], wc[layer, 2]], axis=1)
-            ga[pl.ds(s, b2), :] = nt(taps(gc, s, b2, d, (2, 1, 0)), w)
-
-        @pl.loop(0, rows // 16, unroll=2)
-        def _(b):
-            s = pl.multiple_of(b * 16, 16)
-            x = hidden[pl.ds(pl.multiple_of(s + hoff, 16), 16), :]
-            r = lax.rsqrt(jnp.sum(x * x, axis=1, keepdims=True) * (1.0 / chan) + 1e-06)
-            dn = ga[pl.ds(s, 16), :] * gelu_slope(x * r * gain) * gain
-            m = jnp.sum(dn * x, axis=1, keepdims=True) * (r * r * r * (1.0 / chan))
-            g = grad[pl.ds(s, 16), :] + (dn * r - x * m)
-            if low is None:
-                grad[pl.ds(s, 16), :] = g
-            else:
-                hi = g.astype(BF16)
-                low[0, pl.ds(s, 16), :] = hi
-                low[1, pl.ds(s, 16), :] = (g - hi.astype(F32)).astype(BF16)
+        w = jnp.concatenate([wc[layer, 0], wc[layer, 1], wc[layer, 2]], axis=1)
+        lhs = jnp.concatenate([get(gc, k * d, part) for k in (2, 1, 0)], axis=1)
+        put(ga, 0, part, nt(lhs, w))
+        for first, count in part:
+            @pl.loop(0, count // 16, unroll=2)
+            def _(b):
+                s = pl.multiple_of(first + b * 16, 16)
+                h = pl.multiple_of(s + hoff, 16)
+                x = hidden[pl.ds(h, 16), :]
+                r = scale[pl.ds(h, 16), :][:, 0:1]
+                dn = ga[pl.ds(s, 16), :] * gelu_slope(x * r * gain) * gain
+                m = jnp.sum(dn * x, axis=1, keepdims=True) * (r * r * r * (1.0 / chan))
+                g = grad[pl.ds(s, 16), :] + (dn * r - x * m)
+                if low is None:
+                    grad[pl.ds(s, 16), :] = g
+                else:
+                    hi = g.astype(BF16)
+                    low[0, pl.ds(s, 16), :] = hi
+                    low[1, pl.ds(s, 16), :] = (g - hi.astype(F32)).astype(BF16)
 
     x1 = edge(1, gc1.at[pl.ds(D1, D1), :], gc1.at[pl.ds(D1 + rows, D1), :],
               gc1.at[pl.ds(rows, D1), :], gc1.at[pl.ds(0, D1), :])
+    conv_grad(gc1, D1, 1, co1, 0, ends)
     x1[0]()
-    back(x1, gc1, D1, 1, h1, D1, None)
-
-    @pl.loop(0, 2)
-    def _(b):
-        s = pl.multiple_of(b * b2, 64)
-        gb = nn(grad[pl.ds(s, b2), :].astype(BF16), wp[0])
-        gc0[pl.ds(pl.multiple_of(D0 + s, 32), b2), :] = (gb * gelu_slope(co0[pl.ds(pl.multiple_of(s + D1, 64), b2), :])).astype(BF16)
+    pool_send(cut1, cut2)
+    conv_grad(gc1, D1, 1, co1, 0, middle)
+    back(gc1, D1, 1, h1, r1, D1, None, middle)
+    x1[1]()
+    back(gc1, D1, 1, h1, r1, D1, None, ends)
 
     x0 = edge(2, gc0.at[pl.ds(D0, D0), :], gc0.at[pl.ds(D0 + rows, D0), :],
               gc0.at[pl.ds(rows, D0), :], gc0.at[pl.ds(0, D0), :])
+    conv_grad(gc0, D0, 0, co0, D1, ends)
     x0[0]()
-    back(x0, gc0, D0, 0, h0, e0, glo)
-
-    proj = nt(stem[...], glo[0]) + nt(stem[...], glo[1])
-    pj_s[0] = proj[:, 0:EDGE].astype(BF16)
-    pj_s[1] = proj[:, rows - EDGE:rows].astype(BF16)
+    pool_send(cut2, n)
+    conv_grad(gc0, D0, 0, co0, D1, middle)
+    back(gc0, D0, 0, h0, r0, e0, glo, middle)
+    x0[1]()
+    back(gc0, D0, 0, h0, r0, e0, glo, ends)
+
+    def project(part):
+        return nt(stem[...], get(glo.at[0], 0, part)) + nt(stem[...], get(glo.at[1], 0, part))
+
+    proj_e = project(ends)
+    pj_s[0] = proj_e[:, 0:EDGE].astype(BF16)
+    pj_s[1] = proj_e[:, q + q - EDGE:q + q].astype(BF16)
     xp = edge(3, pj_s.at[0], pj_r, pj_s.at[1], pj_l)
     xp[0]()
+    proj = jnp.concatenate([proj_e[:, 0:q], project(middle), proj_e[:, q:2 * q]], axis=1)
     xp[1]()
     full = jnp.concatenate([pj_l[...].astype(F32), proj, pj_r[...].astype(F32)], axis=1)
     total = jnp.zeros((8, wide), F32)
@@ -329,8 +357,6 @@
     ch, prow = cotangent.shape[1], rows // POOL
     layers, half, taps_n, ff = conv_weight.shape
     chan = 2 * half
-    taps_b = stem_weight.shape[0] * stem_weight.shape[1]
-    stem = jnp.pad(stem_weight.reshape(taps_b, chan), ((0, 64 - taps_b), (0, 0)))
     wconv = conv_weight.transpose(0, 2, 1, 3)
     any_spec = pl.BlockSpec(memory_space=pl.ANY)
     vm = pl.BlockSpec(memory_space=pltpu.VMEM)
@@ -353,6 +379,7 @@
             V((ext1, ff), BF16), V((rows + 2 * D0, ff), BF16), V((2, rows, chan), BF16),
             V((1, EDGE), jnp.int32), V((1, EDGE), jnp.int32),
             V((64, EDGE), BF16), V((64, EDGE), BF16), V((2, 64, EDGE), BF16),
+            V((64, chan), BF16), V((ext0, 128), F32), V((ext1, 128), F32),
             DMA((2 * layers,)), DMA((2 * layers,)), DMA((2 * layers,)),
             DMA((n,)), DMA((n,)), DMA((n,)), DMA((n,)), DMA((2,)),
             DMA((8,)), DMA((8,)),
@@ -360,7 +387,7 @@
         compiler_params=pltpu.CompilerParams(
             collective_id=0, has_side_effects=True, vmem_limit_bytes=56 * 1024 * 1024),
         cost_estimate=pl.CostEstimate(flops=10_000_000_000, bytes_accessed=12_000_000, transcendentals=4_000_000),
-    )(base_codes, stem, norm_gains, wconv, point_weight, cotangent)
+    )(base_codes, stem_weight, norm_gains, wconv, point_weight, cotangent)
 
 
 def solution(mesh):

time: 75.2 us -> 58.6 us (0.78)
  Pallas kernels: 69.2 us -> 54 us
  local copies, waits for them, and re-layouts: 5.05 us -> 3.38 us
    pallas_call x1, Pallas kernels: 69.2 us -> 54 us  [body(): pl.pallas_call(functools.partial(kernel, n), out_shape=(jax.ShapeDtypeStr...]
    reshape x1 -> x0, local copies, waits for them, and re-layouts: 0.97 us -> none  [body(): stem_weight.reshape(taps_b, chan)]
where the time goes in v2:
time: 58.6 us; the launch traced here: 58.1 us
  Pallas kernels  54 us (92%)
  local copies, waits for them, and re-layouts  3.38 us (6%)
  between operations  0.64 us (1%)
    pallas_call x1, Pallas kernels, body(): pl.pallas_call(functools.partial(kernel, n), out_shape=(jax.ShapeDtypeStr...  54 us
    unnamed x2, local copies, waits for them, and re-layouts  3.38 us

profile of v2, /device:TPU:10, one launch (start us, length us, event | category | flops | bytes accessed | tf_op | source)
XLA Modules:
  0.0 58.1 jit_solution(12905274274358269528)
XLA Ops:
  0.6 54.0 %shard_map.77 = (bf16[1,192,2048]{2,1,0:T(8,128)(2,1)}, f32[1,4,512]{2,1,0:T(4,128)}) custom-call(s32[1,512]{1,0:T(1,128)} %codes.1, bf16[15,4,1536]{2,1,0:T(4,128)(2,1)} %stem3.1, f32[2,1536]{1,0:T(2,128)} %gains.1, bf16[2,3,768,384]{3,2,1,0:T(8,128)(2,1)} %bitcast.1, bf16[2,768,384]{2,1,0:T(8,128)(2,1)} %wpoint.1, bf16[1,192,2048]{2,1,0:T(8,128)(2,1)} %cot.1), custom_call_target="tpu_custom_call" | custom-call | flops 10000000000 | bytes 12000000 | tf_op jit(solution)/shard_map/pallas_call | solution.py:366
  54.7 2.1 %copy.10 = bf16[1,192,2048]{2,1,0:T(8,128)(2,1)} copy(bf16[1,192,2048]{2,1,0:T(8,128)(2,1)} %get-tuple-element.4) | data formatting | bytes 1572864
  56.8 1.3 %copy.11 = f32[1,4,512]{2,1,0:T(4,128)} copy(f32[1,4,512]{2,1,0:T(4,128)} %get-tuple-element.5) | data formatting | bytes 16384

commit v3 on v2

--- a/solution.py
+++ b/solution.py
@@ -169,7 +169,7 @@
     def activate(src, dst, scale, count, halo, layer):
         gain = gains[pl.ds(layer, 1), :]
 
-        @pl.loop(0, count // 16, unroll=2)
+        @pl.loop(0, count // 16, unroll=8)
         def _(b):
             s = pl.multiple_of(b * 16, 16)
             x = src[pl.ds(s, 16), :]
@@ -282,7 +282,7 @@
         lhs = jnp.concatenate([get(gc, k * d, part) for k in (2, 1, 0)], axis=1)
         put(ga, 0, part, nt(lhs, w))
         for first, count in part:
-            @pl.loop(0, count // 16, unroll=2)
+            @pl.loop(0, count // 16, unroll=8)
             def _(b):
                 s = pl.multiple_of(first + b * 16, 16)
                 h = pl.multiple_of(s + hoff, 16)

time: 58.6 us -> 54.4 us (0.928)
  Pallas kernels: 54 us -> 50.2 us
    pallas_call x1, Pallas kernels: 54 us -> 50.2 us  [body(): pl.pallas_call(functools.partial(kernel, n), out_shape=(jax.ShapeDtypeStr...]
where the time goes in v3:
time: 54.4 us; the launch traced here: 54.2 us
  Pallas kernels  50.2 us (92%)
  local copies, waits for them, and re-layouts  3.38 us (6%)
  between operations  0.64 us (1%)
    pallas_call x1, Pallas kernels, body(): pl.pallas_call(functools.partial(kernel, n), out_shape=(jax.ShapeDtypeStr...  50.2 us
    unnamed x2, local copies, waits for them, and re-layouts  3.38 us

profile of v3, /device:TPU:10, one launch (start us, length us, event | category | flops | bytes accessed | tf_op | source)
XLA Modules:
  0.0 54.2 jit_solution(2093771814446682779)
XLA Ops:
  0.6 50.2 %shard_map.77 = (bf16[1,192,2048]{2,1,0:T(8,128)(2,1)}, f32[1,4,512]{2,1,0:T(4,128)}) custom-call(s32[1,512]{1,0:T(1,128)} %codes.1, bf16[15,4,1536]{2,1,0:T(4,128)(2,1)} %stem3.1, f32[2,1536]{1,0:T(2,128)} %gains.1, bf16[2,3,768,384]{3,2,1,0:T(8,128)(2,1)} %bitcast.1, bf16[2,768,384]{2,1,0:T(8,128)(2,1)} %wpoint.1, bf16[1,192,2048]{2,1,0:T(8,128)(2,1)} %cot.1), custom_call_target="tpu_custom_call" | custom-call | flops 10000000000 | bytes 12000000 | tf_op jit(solution)/shard_map/pallas_call | solution.py:366
  50.8 2.1 %copy.10 = bf16[1,192,2048]{2,1,0:T(8,128)(2,1)} copy(bf16[1,192,2048]{2,1,0:T(8,128)(2,1)} %get-tuple-element.4) | data formatting | bytes 1572864
  52.9 1.3 %copy.11 = f32[1,4,512]{2,1,0:T(4,128)} copy(f32[1,4,512]{2,1,0:T(4,128)} %get-tuple-element.5) | data formatting | bytes 16384
